TPU v7x, 256 devices: a whole 4x4x8 slice. The times are simulated.
256 devices in a mesh: dp: 32 (over x, y, core), tensor: 8 (over z).
Axes of the slice: x: 4, y: 4, z: 8, core: 2. Of those that a mesh axis runs over, the one named last changes fastest.
Arguments:
- momentum: float32 [32, 5120, 1024], P('dp', None, 'tensor'), may hold values from -6 to 6
- activations: bfloat16 [32768, 5120], P(('dp', 'tensor')), may hold values from -6 to 6
- out_grads: bfloat16 [32768, 1024], P('dp', 'tensor'), may hold values from -0.29882812 to 0.29882812
- positions: int32 [32, 16, 4, 5120], P('dp', 'tensor'), may hold values from 0 to 63, as said below
Outputs:
- new_momentum: float32 [32, 5120, 1024], P('dp', None, 'tensor')
- update: bfloat16 [5120, 1024], P(None, 'tensor')
Inputs may be any that keep to these rules, and one draw needn't show every extreme that they name: The 4 positions of one block of one row of one replica are all different.
All inputs are finite; a program needn't handle non-finite values.
Results may differ from a plain program's by a relative error of at most 0.00075.
Values may be sent and summed in bfloat16 or wider, within the bound.
A program may use at most 128 MiB of HBM per device.

v0:
```python
import jax
import jax.numpy as jnp
from jax import lax
from jax.sharding import PartitionSpec as P


def sent_to_all(value, axis):
    copies = jnp.broadcast_to(value, (lax.axis_size(axis), *value.shape))
    return lax.all_to_all(copies, axis, split_axis=0, concat_axis=0, tiled=True)


def over_copies(value, axis):
    everything = sent_to_all(value, axis)
    return jnp.sum(everything, axis=0)


def dct_table():
    freq = jnp.arange(64, dtype=jnp.float32)[:, None]
    place = jnp.arange(64, dtype=jnp.float32)[None, :]
    scales = jnp.where(freq == 0, jnp.float32(1.0 / 8.0), jnp.float32((2.0 / 64.0) ** 0.5))
    return scales * jnp.cos(jnp.float32(jnp.pi) * (2.0 * place + 1.0) * freq / 128.0)


def body(momentum, activations, out_grads, positions):
    width = momentum.shape[1]
    local_cols = momentum.shape[2]
    spans = local_cols // 64
    blocks = jnp.kron(jnp.eye(spans, dtype=jnp.float32), dct_table())
    lane_ids = jnp.arange(64, dtype=jnp.int32)[None, :, None]
    gradient = lax.dot_general(
        out_grads,
        lax.all_gather(activations, "tensor", axis=0, tiled=True),
        (((0,), (0,)), ((), ())),
        preferred_element_type=jnp.float32,
    )
    accumulated = 0.9 * momentum[0].T + gradient
    coeffs = jnp.dot(blocks, accumulated, precision=lax.Precision.HIGHEST).reshape(spans, 64, width)
    picks = positions[0]
    chosen = jnp.zeros((spans, 64, width), jnp.float32)
    value_list = []
    for slot in range(4):
        hits = picks[:, slot, None, :] == lane_ids
        chosen = chosen + jnp.where(hits, 1.0, 0.0)
        value_list.append(jnp.sum(jnp.where(hits, coeffs, 0.0), axis=1))
    own_tile = coeffs * chosen
    restored = jnp.dot(
        blocks.T, own_tile.reshape(local_cols, width), precision=lax.Precision.HIGHEST
    )
    new_momentum = (accumulated - restored).T
    summed = lax.psum(own_tile.reshape(local_cols, width), "dp")
    decoded = jnp.dot(blocks.T, summed, precision=lax.Precision.HIGHEST)
    row_squares = over_copies(jnp.sum(decoded * decoded, axis=0), "tensor")
    row_scale = jnp.sqrt(row_squares / (local_cols * lax.axis_size("tensor")) + 1e-05)
    update = (decoded / row_scale[None, :]).T.astype(jnp.bfloat16)
    return (new_momentum[None], update)


def solution(mesh):
    placed = (
        P("dp", None, "tensor"),
        P(("dp", "tensor"), None),
        P("dp", "tensor"),
        P("dp", "tensor", None, None),
    )
    return jax.shard_map(
        body,
        mesh=mesh,
        in_specs=placed,
        out_specs=(P("dp", None, "tensor"), P(None, "tensor")),
        check_vma=False,
    )
```

profile of v0, /device:TPU:6, one launch (start us, length us, event | category | flops | bytes accessed | tf_op | source)
XLA Modules:
  0.0 300.0 jit_solution(9160599858302777899)
XLA Ops:
  7.2 0.0 all-gather.2.cloned.1.call-start
  7.2 0.7 all-gather.2.cloned.1.call-update
  7.9 0.1 mul.156
  8.0 0.1 mul.157
  8.1 0.1 cosine_multiply_fusion
  8.3 0.1 mul.169
  8.4 0.1 broadcast_multiply_fusion
  8.5 0.1 mul.177
  8.6 2.2 copy.14
  10.8 0.1 fusion.10
  11.0 115.5 %all-gather.2.cloned.1.call-done = bf16[1024,5120]{1,0:T(8,128)(2,1)} async-done(((bf16[128,5120]{1,0:T(8,128)(2,1)}), bf16[1024,5120]{1,0:T(8,128)(2,1)}) %all-gather.2.cloned.1.call-update) | async-done | bytes 10485776 | tf_op jit(solution)/shard_map/all_gather | solution.py:32
  126.5 5.5 %fusion.11 = f32[128,5120]{1,0:T(8,128)S(1)} fusion(bf16[1024,128]{1,0:T(8,128)(2,1)S(1)} %copy-done, bf16[1024,5120]{1,0:T(8,128)(2,1)} %all-gather.2.cloned.1.call-done), kind=kOutput, calls=%fused_computation.30 | convolution fusion | flops 1342177280 | bytes 13369344 | tf_op jit(solution)/shard_map/dot_general | solution.py:30
  132.1 5.0 %convolution_multiply_fusion = f32[2,64,5120]{2,1,0:T(8,128)} fusion(f32[128,5120]{1,0:T(8,128)S(1)} %fusion.11, f32[1,5120,128]{1,2,0:T(8,128)S(1)} %copy.14, s32[2,5120]{1,0:T(2,128)S(1)} %get-tuple-element.14, s32[2,5120]{1,0:T(2,128)S(1)} %get-tuple-element.15, s32[2,5120]{1,0:T(2,128)S(1)} %get-tuple-element.16, s32[2,5120]{1,0:T(2,128)S(1)} %get-tuple-element.17, ...), kind=kOutput, calls=%fused_computation.2 | convolution fusion | flops 1015824384 | bytes 8061952 | tf_op jit(solution)/shard_map/dot_general | solution.py:37
  137.1 6.8 %fusion = f32[1,5120,128]{1,2,0:T(8,128)} fusion(f32[128,5120]{1,0:T(8,128)} %bitcast.35, f32[128,128]{1,0:T(8,128)S(1)} %mul.177, f32[128,5120]{1,0:T(8,128)} %copy-done.2, f32[1,5120,128]{1,2,0:T(8,128)S(1)} %copy.14), kind=kOutput, calls=%fused_computation.1 | convolution fusion | flops 1008599040 | bytes 10551296 | tf_op jit(solution)/shard_map/dot_general | solution.py:46
  144.0 0.7 all-reduce.2.cloned.1.call-update
  144.7 122.1 %all-reduce.2.cloned.1.call-done = f32[128,5120]{1,0:T(8,128)} async-done(((f32[128,5120]{1,0:T(8,128)}), f32[128,5120]{1,0:T(8,128)}) %all-reduce.2.cloned.1.call-update) | async-done | bytes 2621456 | tf_op jit(solution)/shard_map/psum | solution.py:50
  266.8 5.7 %multiply_reduce_fusion = (f32[5120]{0:T(1024)S(1)}, f32[128,5120]{1,0:T(8,128)}) fusion(f32[128,128]{1,0:T(8,128)S(1)} %mul.177, f32[128,5120]{1,0:T(8,128)} %all-reduce.2.cloned.1.call-done), kind=kOutput, calls=%fused_computation.7 | convolution fusion | flops 1007938560 | bytes 5328896 | tf_op jit(solution)/shard_map/dot_general | solution.py:51
  272.4 0.8 broadcast_in_dim.41
  273.2 7.0 %all-to-all-start = ((f32[8,1,5120]{2,1,0:T(1,128)}), f32[8,1,5120]{2,1,0:T(1,128)S(1)}, u32[]{:S(2)}, u32[]{:S(2)}) async-start(f32[8,1,5120]{2,1,0:T(1,128)} %broadcast_in_dim.41), calls=%async_computation | async-start | bytes 327680 | tf_op jit(solution)/shard_map/all_to_all | solution.py:9
  280.2 2.1 copy.17
  282.3 7.3 %all-to-all-done = f32[8,1,5120]{2,1,0:T(1,128)S(1)} async-done(((f32[8,1,5120]{2,1,0:T(1,128)}), f32[8,1,5120]{2,1,0:T(1,128)S(1)}, u32[]{:S(2)}, u32[]{:S(2)}) %all-to-all-start) | async-done | bytes 163872 | tf_op jit(solution)/shard_map/all_to_all | solution.py:9
  289.6 0.1 reduce_sum.19
  289.8 1.9 fusion.5
  291.7 1.4 copy.18
  (15 shorter events, 0.2 us)
Async XLA Ops:
  7.2 119.4 %copy-start = (bf16[1024,128]{1,0:T(8,128)(2,1)S(1)}, bf16[1024,128]{1,0:T(8,128)(2,1)}, u32[]{:S(2)}) copy-start(bf16[1024,128]{1,0:T(8,128)(2,1)} %param.6) | copy-start | bytes 786436
  7.2 119.4 %all-gather.2.cloned.1.call-start = ((), (), s32[]{:S(2)}) async-start(), calls=%async_computation.1 | async-start | bytes 11796480 | tf_op jit(solution)/shard_map/all_gather | solution.py:32
  8.6 2.2 copy-start.3
  132.1 5.0 %copy-start.2 = (f32[128,5120]{1,0:T(8,128)}, f32[128,5120]{1,0:T(8,128)S(1)}, u32[]{:S(2)}) copy-start(f32[128,5120]{1,0:T(8,128)S(1)} %fusion.11) | copy-start | bytes 7864324
  144.0 122.8 %all-reduce.2.cloned.1.call-start = ((), (), s32[]{:S(2)}) async-start(), calls=%async_computation.2 | async-start | bytes 5242880 | tf_op jit(solution)/shard_map/psum | solution.py:50
  144.7 135.5 %copy-start.1 = (f32[1,5120,128]{1,2,0:T(8,128)S(1)}, f32[1,5120,128]{1,2,0:T(8,128)}, u32[]{:S(2)}) copy-start(f32[1,5120,128]{1,2,0:T(8,128)} %fusion) | copy-start | bytes 7864324
  273.2 16.4 %all-to-all-start = ((f32[8,1,5120]{2,1,0:T(1,128)}), f32[8,1,5120]{2,1,0:T(1,128)S(1)}, u32[]{:S(2)}, u32[]{:S(2)}) async-start(f32[8,1,5120]{2,1,0:T(1,128)} %broadcast_in_dim.41), calls=%async_computation | async-start | bytes 327680 | tf_op jit(solution)/shard_map/all_to_all | solution.py:9
Sparse Core Ops, SparseCore 0:
  9.8 116.6 all-gather.1
  148.6 118.0 all-reduce.1
where the time goes:
time: 300 us
  waiting for transfers between devices  246 us (82%)
  matrix products  23 us (8%)
  between operations  14.1 us (5%)
  local copies, waits for them, and re-layouts  7.1 us (2%)
  starting transfers between devices  7.05 us (2%)
    psum x1, waiting for transfers between devices, body(): summed = lax.psum(own_tile.reshape(local_cols, width), 'dp')  122 us
    all_gather x1, waiting for transfers between devices, body(): lax.all_gather(activations, 'tensor', axis=0, tiled=True)  116 us
    all_to_all x1, waiting for transfers between devices, sent_to_all(): return lax.all_to_all(copies, axis, split_axis=0, concat_axis=0, tiled=True)  7.34 us
    all_to_all x1, starting transfers between devices, sent_to_all(): return lax.all_to_all(copies, axis, split_axis=0, concat_axis=0, tiled=True)  7.01 us
    dot_general x1, matrix products, body(): jnp.dot(blocks.T, own_tile.reshape(local_cols, width), precision=lax.Prec...  6.83 us
  transfers between devices with their start and end apart: 3, of which 3 were waited for; matrix products, arithmetic and copies ran while one was open for 2% of the time, Pallas kernels for 0%

commit v1 on v0

--- a/solution.py
+++ b/solution.py
@@ -47,7 +47,7 @@
         blocks.T, own_tile.reshape(local_cols, width), precision=lax.Precision.HIGHEST
     )
     new_momentum = (accumulated - restored).T
-    summed = lax.psum(own_tile.reshape(local_cols, width), "dp")
+    summed = jnp.sum(lax.all_gather(own_tile.reshape(local_cols, width), "dp"), axis=0)
     decoded = jnp.dot(blocks.T, summed, precision=lax.Precision.HIGHEST)
     row_squares = over_copies(jnp.sum(decoded * decoded, axis=0), "tensor")
     row_scale = jnp.sqrt(row_squares / (local_cols * lax.axis_size("tensor")) + 1e-05)

time: 300 us -> 444 us (1.48)
  waiting for transfers between devices: 246 us -> 367 us
  other arithmetic: 2.34 us -> 28.1 us
    all_gather x0 -> x1, waiting for transfers between devices: none -> 248 us  [body(): lax.all_gather(own_tile.reshape(local_cols, width), 'dp')]
    psum x1 -> x0, waiting for transfers between devices: 122 us -> none  [body(): summed = lax.psum(own_tile.reshape(local_cols, width), 'dp')]
    reduce_sum x0 -> x1, other arithmetic: none -> 25.8 us  [body(): jnp.sum(lax.all_gather(own_tile.reshape(local_cols, width), 'dp'), axis=0)]
    all_to_all x1, waiting for transfers between devices: 7.34 us -> 2 us  [sent_to_all(): return lax.all_to_all(copies, axis, split_axis=0, concat_axis=0, tiled=True)]
  transfers between devices with their start and end apart: 3 -> 3, of which waited for: 3 -> 3; matrix products, arithmetic and copies ran while one was open for 2% -> 3% of each run, Pallas kernels for 0% -> 0%
where the time goes in v1:
time: 444 us
  waiting for transfers between devices  367 us (83%)
  other arithmetic  28.1 us (6%)
  matrix products  20.6 us (5%)
  between operations  14.2 us (3%)
  local copies, waits for them, and re-layouts  7.1 us (2%)
  starting transfers between devices  7.09 us (2%)
    all_gather x1, waiting for transfers between devices, body(): lax.all_gather(own_tile.reshape(local_cols, width), 'dp')  248 us
    all_gather x1, waiting for transfers between devices, body(): lax.all_gather(activations, 'tensor', axis=0, tiled=True)  116 us
    reduce_sum x1, other arithmetic, body(): jnp.sum(lax.all_gather(own_tile.reshape(local_cols, width), 'dp'), axis=0)  25.8 us
  transfers between devices with their start and end apart: 3, of which 3 were waited for; matrix products, arithmetic and copies ran while one was open for 3% of the time, Pallas kernels for 0%

profile of v1, /device:TPU:6, one launch (start us, length us, event | category | flops | bytes accessed | tf_op | source)
XLA Modules:
  0.0 443.7 jit_solution(12578821178633660963)
XLA Ops:
  7.2 0.7 all-gather.3.cloned.1.call-update
  7.9 0.0 all-gather.5.cloned.1.call-start
  8.0 0.1 mul.156
  8.0 0.1 mul.157
  8.1 0.1 cosine_multiply_fusion
  8.3 0.1 mul.169
  8.4 2.2 copy.18
  10.6 0.1 fusion.10
  10.9 115.7 %all-gather.3.cloned.1.call-done = bf16[1024,5120]{1,0:T(8,128)(2,1)} async-done(((bf16[128,5120]{1,0:T(8,128)(2,1)}), bf16[1024,5120]{1,0:T(8,128)(2,1)}) %all-gather.3.cloned.1.call-update) | async-done | bytes 10485776 | tf_op jit(solution)/shard_map/all_gather | solution.py:32
  126.5 5.5 %fusion.11 = f32[128,5120]{1,0:T(8,128)S(1)} fusion(bf16[1024,128]{1,0:T(8,128)(2,1)S(1)} %copy-done, bf16[1024,5120]{1,0:T(8,128)(2,1)} %all-gather.3.cloned.1.call-done), kind=kOutput, calls=%fused_computation.30 | convolution fusion | flops 1342177280 | bytes 13369344 | tf_op jit(solution)/shard_map/dot_general | solution.py:30
  132.1 5.0 %convolution_multiply_fusion = f32[2,64,5120]{2,1,0:T(8,128)} fusion(f32[128,5120]{1,0:T(8,128)S(1)} %fusion.11, f32[1,5120,128]{1,2,0:T(8,128)S(1)} %copy.18, s32[2,5120]{1,0:T(2,128)S(1)} %get-tuple-element.16, s32[2,5120]{1,0:T(2,128)S(1)} %get-tuple-element.17, s32[2,5120]{1,0:T(2,128)S(1)} %get-tuple-element.18, s32[2,5120]{1,0:T(2,128)S(1)} %get-tuple-element.19, ...), kind=kOutput, calls=%fused_computation.2 | convolution fusion | flops 1015824384 | bytes 8061952 | tf_op jit(solution)/shard_map/dot_general | solution.py:37
  137.1 0.1 broadcast_multiply_fusion
  137.3 0.1 mul.177
  137.4 248.2 %all-gather.5.cloned.1.call-done = f32[32,128,5120]{2,1,0:T(8,128)} async-done(((f32[1,128,5120]{2,1,0:T(8,128)}), f32[32,128,5120]{2,1,0:T(8,128)}) %all-gather.5.cloned.1.call-update) | async-done | bytes 83886096 | tf_op jit(solution)/shard_map/all_gather | solution.py:50
  385.6 25.8 %reduce_sum.27 = f32[128,5120]{1,0:T(8,128)S(1)} reduce(f32[32,128,5120]{2,1,0:T(8,128)} %all-gather.5.cloned.1.call-done, f32[]{:T(128)} %constant.11.clone.1), dimensions={0}, to_apply=%region_0.1 | reduce | flops 20316160 | bytes 86507520 | tf_op jit(solution)/shard_map/reduce_sum | solution.py:50
  411.4 4.0 multiply_reduce_fusion
  415.4 0.8 broadcast_in_dim.41
  416.1 7.0 %all-to-all-start = ((f32[8,1,5120]{2,1,0:T(1,128)}), f32[8,1,5120]{2,1,0:T(1,128)S(1)}, u32[]{:S(2)}, u32[]{:S(2)}) async-start(f32[8,1,5120]{2,1,0:T(1,128)} %broadcast_in_dim.41), calls=%async_computation | async-start | bytes 327680 | tf_op jit(solution)/shard_map/all_to_all | solution.py:9
  423.1 6.1 %fusion = f32[1,5120,128]{1,2,0:T(8,128)S(1)} fusion(f32[128,5120]{1,0:T(8,128)} %bitcast.37, f32[128,128]{1,0:T(8,128)S(1)} %mul.177, f32[128,5120]{1,0:T(8,128)} %copy-done.2, f32[1,5120,128]{1,2,0:T(8,128)} %copy-done.1), kind=kOutput, calls=%fused_computation.1 | convolution fusion | flops 1008599040 | bytes 10551296 | tf_op jit(solution)/shard_map/dot_general | solution.py:46
  429.2 2.1 copy.21
  431.3 2.0 all-to-all-done
  433.3 0.1 reduce_sum.29
  433.5 1.9 fusion.5
  435.4 1.4 copy.22
  (16 shorter events, 0.2 us)
Async XLA Ops:
  7.2 119.4 %copy-start = (bf16[1024,128]{1,0:T(8,128)(2,1)S(1)}, bf16[1024,128]{1,0:T(8,128)(2,1)}, u32[]{:S(2)}) copy-start(bf16[1024,128]{1,0:T(8,128)(2,1)} %param.6) | copy-start | bytes 786436
  7.2 119.4 %all-gather.3.cloned.1.call-start = ((), (), s32[]{:S(2)}) async-start(), calls=%async_computation.1 | async-start | bytes 11796480 | tf_op jit(solution)/shard_map/all_gather | solution.py:32
  7.9 377.7 %all-gather.5.cloned.1.call-start = ((), (), s32[]{:S(2)}) async-start(), calls=%async_computation.2 | async-start | bytes 86507520 | tf_op jit(solution)/shard_map/all_gather | solution.py:50
  8.4 2.2 copy-start.3
  10.6 121.5 %copy-start.1 = (f32[1,5120,128]{1,2,0:T(8,128)}, f32[1,5120,128]{1,2,0:T(8,128)S(1)}, u32[]{:S(2)}) copy-start(f32[1,5120,128]{1,2,0:T(8,128)S(1)} %copy.18) | copy-start | bytes 7864324
  132.1 5.0 %copy-start.2 = (f32[128,5120]{1,0:T(8,128)}, f32[128,5120]{1,0:T(8,128)S(1)}, u32[]{:S(2)}) copy-start(f32[128,5120]{1,0:T(8,128)S(1)} %fusion.11) | copy-start | bytes 7864324
  416.1 17.2 %all-to-all-start = ((f32[8,1,5120]{2,1,0:T(1,128)}), f32[8,1,5120]{2,1,0:T(1,128)S(1)}, u32[]{:S(2)}, u32[]{:S(2)}) async-start(f32[8,1,5120]{2,1,0:T(1,128)} %broadcast_in_dim.41), calls=%async_computation | async-start | bytes 327680 | tf_op jit(solution)/shard_map/all_to_all | solution.py:9
Sparse Core Ops, SparseCore 0:
  9.8 116.6 all-gather.2
  137.3 248.2 all-gather.4

commit v2 on v0

--- a/solution.py
+++ b/solution.py
@@ -29,7 +29,10 @@
     lane_ids = jnp.arange(64, dtype=jnp.int32)[None, :, None]
     gradient = lax.dot_general(
         out_grads,
-        lax.all_gather(activations, "tensor", axis=0, tiled=True),
+        jnp.concatenate(
+            lax.all_to_all(jnp.stack([activations] * lax.axis_size("tensor")), "tensor", 0, 0),
+            axis=0,
+        ),
         (((0,), (0,)), ((), ())),
         preferred_element_type=jnp.float32,
     )

time: 300 us -> 426 us (1.42)
  waiting for transfers between devices: 246 us -> 356 us
  starting transfers between devices: 7.05 us -> 15.5 us
  local copies, waits for them, and re-layouts: 7.1 us -> 13.7 us
    all_to_all x0 -> x1, waiting for transfers between devices: none -> 229 us  [body(): lax.all_to_all(jnp.stack([activations] * lax.axis_size('tensor')), 'tenso...]
    all_gather x1 -> x0, waiting for transfers between devices: 116 us -> none  [body(): lax.all_gather(activations, 'tensor', axis=0, tiled=True)]
    all_to_all x0 -> x1, starting transfers between devices: none -> 8.47 us  [body(): lax.all_to_all(jnp.stack([activations] * lax.axis_size('tensor')), 'tenso...]
    another operation x0 -> x1, local copies, waits for them, and re-layouts: none -> 6.61 us  [body(): jnp.stack([activations] * lax.axis_size('tensor'))]
  transfers between devices with their start and end apart: 3 -> 3, of which waited for: 3 -> 3; matrix products, arithmetic and copies ran while one was open for 2% -> 1% of each run, Pallas kernels for 0% -> 0%
where the time goes in v2:
time: 426 us; the launch traced here: 425 us
  waiting for transfers between devices  356 us (84%)
  matrix products  23.1 us (5%)
  starting transfers between devices  15.5 us (4%)
  between operations  14.1 us (3%)
  local copies, waits for them, and re-layouts  13.7 us (3%)
    all_to_all x1, waiting for transfers between devices, body(): lax.all_to_all(jnp.stack([activations] * lax.axis_size('tensor')), 'tenso...  229 us
    psum x1, waiting for transfers between devices, body(): summed = lax.psum(own_tile.reshape(local_cols, width), 'dp')  120 us
  transfers between devices with their start and end apart: 3, of which 3 were waited for; matrix products, arithmetic and copies ran while one was open for 1% of the time, Pallas kernels for 0%

profile of v2, /device:TPU:6, one launch (start us, length us, event | category | flops | bytes accessed | tf_op | source)
XLA Modules:
  0.0 425.1 jit_solution(11240028483005151149)
XLA Ops:
  7.2 6.6 %stack.2 = bf16[8,128,5120]{2,1,0:T(8,128)(2,1)} broadcast(bf16[128,5120]{1,0:T(8,128)(2,1)} %param.5), dimensions={1,2} | broadcast | bytes 11796480 | tf_op jit(solution)/shard_map/stack | solution.py:33
  13.8 8.5 %all-to-all-start = ((bf16[8,128,5120]{2,1,0:T(8,128)(2,1)}), bf16[8,128,5120]{2,1,0:T(8,128)(2,1)}, u32[]{:S(2)}, u32[]{:S(2)}) async-start(bf16[8,128,5120]{2,1,0:T(8,128)(2,1)} %stack.2), calls=%async_computation | async-start | bytes 20971520 | tf_op jit(solution)/shard_map/all_to_all | solution.py:33
  22.3 2.2 copy.14
  24.5 0.1 cosine_multiply_fusion
  24.6 0.1 mul.169
  24.8 0.1 mul.156
  24.8 0.1 mul.157
  24.9 0.1 broadcast_multiply_fusion
  25.0 0.1 mul.177
  25.2 0.1 fusion.10
  25.4 228.6 %all-to-all-done = bf16[8,128,5120]{2,1,0:T(8,128)(2,1)} async-done(((bf16[8,128,5120]{2,1,0:T(8,128)(2,1)}), bf16[8,128,5120]{2,1,0:T(8,128)(2,1)}, u32[]{:S(2)}, u32[]{:S(2)}) %all-to-all-start) | async-done | bytes 10485792 | tf_op jit(solution)/shard_map/all_to_all | solution.py:33
  254.0 5.5 %fusion.11 = f32[128,5120]{1,0:T(8,128)S(1)} fusion(bf16[1024,128]{1,0:T(8,128)(2,1)S(1)} %copy-done, bf16[1024,5120]{1,0:T(8,128)(2,1)} %bitcast.1), kind=kOutput, calls=%fused_computation.30 | convolution fusion | flops 1342177280 | bytes 13369344 | tf_op jit(solution)/shard_map/dot_general | solution.py:30
  259.6 5.0 %convolution_multiply_fusion = f32[2,64,5120]{2,1,0:T(8,128)} fusion(f32[128,5120]{1,0:T(8,128)S(1)} %fusion.11, f32[1,5120,128]{1,2,0:T(8,128)S(1)} %copy.14, s32[2,5120]{1,0:T(2,128)S(1)} %get-tuple-element.14, s32[2,5120]{1,0:T(2,128)S(1)} %get-tuple-element.15, s32[2,5120]{1,0:T(2,128)S(1)} %get-tuple-element.16, s32[2,5120]{1,0:T(2,128)S(1)} %get-tuple-element.17, ...), kind=kOutput, calls=%fused_computation.2 | convolution fusion | flops 1015824384 | bytes 8061952 | tf_op jit(solution)/shard_map/dot_general | solution.py:40
  264.6 6.8 %fusion = f32[1,5120,128]{1,2,0:T(8,128)} fusion(f32[128,5120]{1,0:T(8,128)} %bitcast.36, f32[128,128]{1,0:T(8,128)S(1)} %mul.177, f32[128,5120]{1,0:T(8,128)} %copy-done.2, f32[1,5120,128]{1,2,0:T(8,128)S(1)} %copy.14), kind=kOutput, calls=%fused_computation.1 | convolution fusion | flops 1008599040 | bytes 10551296 | tf_op jit(solution)/shard_map/dot_general | solution.py:49
  271.4 0.7 all-reduce.2.cloned.1.call-update
  272.1 119.8 %all-reduce.2.cloned.1.call-done = f32[128,5120]{1,0:T(8,128)} async-done(((f32[128,5120]{1,0:T(8,128)}), f32[128,5120]{1,0:T(8,128)}) %all-reduce.2.cloned.1.call-update) | async-done | bytes 2621456 | tf_op jit(solution)/shard_map/psum | solution.py:53
  391.9 5.7 %multiply_reduce_fusion = (f32[5120]{0:T(1024)S(1)}, f32[128,5120]{1,0:T(8,128)}) fusion(f32[128,128]{1,0:T(8,128)S(1)} %mul.177, f32[128,5120]{1,0:T(8,128)} %all-reduce.2.cloned.1.call-done), kind=kOutput, calls=%fused_computation.7 | convolution fusion | flops 1007938560 | bytes 5328896 | tf_op jit(solution)/shard_map/dot_general | solution.py:54
  397.6 0.8 broadcast_in_dim.41
  398.3 7.0 %all-to-all-start.1 = ((f32[8,1,5120]{2,1,0:T(1,128)}), f32[8,1,5120]{2,1,0:T(1,128)S(1)}, u32[]{:S(2)}, u32[]{:S(2)}) async-start(f32[8,1,5120]{2,1,0:T(1,128)} %broadcast_in_dim.41), calls=%async_computation.1 | async-start | bytes 327680 | tf_op jit(solution)/shard_map/all_to_all | solution.py:9
  405.3 2.1 copy.17
  407.4 7.3 %all-to-all-done.1 = f32[8,1,5120]{2,1,0:T(1,128)S(1)} async-done(((f32[8,1,5120]{2,1,0:T(1,128)}), f32[8,1,5120]{2,1,0:T(1,128)S(1)}, u32[]{:S(2)}, u32[]{:S(2)}) %all-to-all-start.1) | async-done | bytes 163872 | tf_op jit(solution)/shard_map/all_to_all | solution.py:9
  414.8 0.1 reduce_sum.19
  414.9 1.9 fusion.5
  416.9 1.4 copy.18
  (15 shorter events, 0.2 us)
Async XLA Ops:
  7.2 246.8 %copy-start = (bf16[1024,128]{1,0:T(8,128)(2,1)S(1)}, bf16[1024,128]{1,0:T(8,128)(2,1)}, u32[]{:S(2)}) copy-start(bf16[1024,128]{1,0:T(8,128)(2,1)} %param.6) | copy-start | bytes 786436
  13.8 240.2 %all-to-all-start = ((bf16[8,128,5120]{2,1,0:T(8,128)(2,1)}), bf16[8,128,5120]{2,1,0:T(8,128)(2,1)}, u32[]{:S(2)}, u32[]{:S(2)}) async-start(bf16[8,128,5120]{2,1,0:T(8,128)(2,1)} %stack.2), calls=%async_computation | async-start | bytes 20971520 | tf_op jit(solution)/shard_map/all_to_all | solution.py:33
  22.3 2.9 copy-start.3
  259.5 5.0 %copy-start.2 = (f32[128,5120]{1,0:T(8,128)}, f32[128,5120]{1,0:T(8,128)S(1)}, u32[]{:S(2)}) copy-start(f32[128,5120]{1,0:T(8,128)S(1)} %fusion.11) | copy-start | bytes 7864324
  271.4 120.5 %all-reduce.2.cloned.1.call-start = ((), (), s32[]{:S(2)}) async-start(), calls=%async_computation.2 | async-start | bytes 5242880 | tf_op jit(solution)/shard_map/psum | solution.py:53
  272.1 133.2 %copy-start.1 = (f32[1,5120,128]{1,2,0:T(8,128)S(1)}, f32[1,5120,128]{1,2,0:T(8,128)}, u32[]{:S(2)}) copy-start(f32[1,5120,128]{1,2,0:T(8,128)} %fusion) | copy-start | bytes 7864324
  398.3 16.4 %all-to-all-start.1 = ((f32[8,1,5120]{2,1,0:T(1,128)}), f32[8,1,5120]{2,1,0:T(1,128)S(1)}, u32[]{:S(2)}, u32[]{:S(2)}) async-start(f32[8,1,5120]{2,1,0:T(1,128)} %broadcast_in_dim.41), calls=%async_computation.1 | async-start | bytes 327680 | tf_op jit(solution)/shard_map/all_to_all | solution.py:9
Sparse Core Ops, SparseCore 0:
  276.1 115.7 all-reduce.1
